TPU v7x, 32 devices: a whole 2x2x4 slice. The times are simulated.
32 devices in a mesh: lat: 16 (over z, y, x), mem: 2 (over core).
Axes of the slice: x: 2, y: 2, z: 4, core: 2. Of those that a mesh axis runs over, the one named last changes fastest.
Arguments:
- obs_rows: float32 [16384, 32], P(('lat', 'mem')), may hold values from -0.18 to 0.18
- obs_band: int32 [16384, 1], P(('lat', 'mem')), may hold values from 0 to 15; in each aligned block of 512 rows (0 to 511, 512 to 1023, ...) at most 32 rows name the same one
- obs_cell: int32 [16384], P(('lat', 'mem')), may hold values from 0 to 1439
- obs_top: int32 [16384], P(('lat', 'mem')), may hold values from 1 to 32
- perturb: bfloat16 [16, 1440, 256], P('lat', None, 'mem'), may hold values from -6 to 6
- control: bfloat16 [16, 1440, 256], P('lat', None, 'mem'), may hold values from -6 to 6
Outputs:
- gradient: float32 [16, 1440, 256], P('lat', None, 'mem')
Inputs may be any that keep to these rules, and one draw needn't show every extreme that they name: `obs_band`: the 512 profiles of one device name one band each; no band is named by more than 32 profiles of one device. `obs_cell`: row within the band times 1440 plus the longitude column. `obs_top`: levels below this index carry the profile; the rest are unused.
All inputs are finite; a program needn't handle non-finite values.
Results may differ from a plain program's by a relative error of at most 0.0003.
Values sent between devices are 32-bit elements; how exact they have to be, the bound alone decides.
A program may use at most 64 MiB of HBM per device.

v0:
```python
import jax
import jax.numpy as jnp
from jax import lax
from jax.sharding import PartitionSpec as P

CAP = 32


def kernel(count, spread, periodic):
    positions = jnp.arange(count, dtype=jnp.float32)
    distance = jnp.abs(positions[:, None] - positions[None, :])
    if periodic:
        distance = jnp.minimum(distance, count - distance)
    return jnp.exp(-0.5 * (distance / spread) ** 2)


def bucket(profiles, band_index, cell_index, top_level, capacity, band_count):
    levels = profiles.shape[1]
    level_mask = (jnp.arange(levels, dtype=jnp.int32)[None, :] < top_level[:, None]).astype(
        jnp.float32
    )
    onehot = (band_index[:, None] == jnp.arange(band_count, dtype=jnp.int32)[None, :]).astype(
        jnp.int32
    )
    earlier = jnp.cumsum(onehot, axis=0) - onehot
    slot_rank = jnp.sum(earlier * onehot, axis=1)
    target_slot = band_index * capacity + slot_rank
    send_rows = (
        jnp.zeros((band_count * capacity, levels), jnp.float32)
        .at[target_slot]
        .set(profiles * level_mask)
    )
    send_cells = jnp.full((band_count * capacity,), -1, jnp.int32).at[target_slot].set(cell_index)
    return (
        send_rows.reshape(band_count, capacity, levels),
        send_cells.reshape(band_count, capacity),
    )


def deposit(got_rows, got_cells, band_cells):
    levels = got_rows.shape[-1]
    flat_rows = got_rows.reshape(-1, levels)
    flat_cells = got_cells.reshape(-1)
    target_cell = jnp.where(flat_cells >= 0, flat_cells, 0)
    return jnp.zeros((band_cells, levels), jnp.float32).at[target_cell].add(flat_rows)


def zonal_rows(field, row_ids, all_rows):
    lon_count = field.shape[1]
    base = float(max(lon_count // 60, 4))

    def one_row(pair):
        row_field, row_id = pair
        latitude = 1.2 * (row_id.astype(jnp.float32) + 0.5) / all_rows
        lonk = kernel(lon_count, base / jnp.cos(latitude), True)
        return jnp.dot(
            lonk, row_field, precision=lax.Precision.HIGHEST, preferred_element_type=jnp.float32
        )

    return lax.map(one_row, (field, row_ids))


def local(obs_rows, obs_band, obs_cell, obs_top, perturb, control):
    band_count = lax.axis_size("lat")
    lat_dev, lon_count, columns = perturb.shape
    levels = obs_rows.shape[1]
    members = columns // levels
    band_cells = lat_dev * lon_count
    all_rows = lat_dev * band_count
    row_ids = lax.axis_index("lat") * lat_dev + jnp.arange(lat_dev, dtype=jnp.int32)
    send_rows, send_cells = bucket(obs_rows, obs_band[:, 0], obs_cell, obs_top, CAP, band_count)
    got_rows, got_cells = (
        lax.all_to_all(send_rows, "lat", split_axis=0, concat_axis=0, tiled=True),
        lax.all_to_all(send_cells, "lat", split_axis=0, concat_axis=0, tiled=True),
    )
    partial_grid = deposit(got_rows, got_cells, band_cells)
    innovation = lax.psum(partial_grid, "mem")
    innovation = innovation.reshape(lat_dev, lon_count, 1, levels)
    product = perturb.reshape(lat_dev, lon_count, members, levels).astype(jnp.float32) * innovation
    product = product.reshape(band_cells, columns)
    column_ids = jnp.arange(columns, dtype=jnp.int32)
    level_pos = (column_ids % levels).astype(jnp.float32)
    same_member = (column_ids[:, None] // levels == column_ids[None, :] // levels).astype(
        jnp.float32
    )
    vert_spread = 1.0
    block_vert = same_member * jnp.exp(
        -0.5 * (jnp.abs(level_pos[:, None] - level_pos[None, :]) / vert_spread) ** 2
    )
    vertical = jnp.dot(
        product, block_vert, precision=lax.Precision.HIGHEST, preferred_element_type=jnp.float32
    )
    vertical = vertical.reshape(lat_dev, lon_count, columns)
    latk = kernel(all_rows, 8.0 * lat_dev, False)
    pieces = vertical.reshape(lat_dev, band_count, lon_count * columns // band_count)
    smoothed = jnp.einsum(
        "rR,Rgc->rgc",
        latk,
        lax.all_to_all(pieces, "lat", split_axis=1, concat_axis=0, tiled=True),
        precision=lax.Precision.HIGHEST,
    )
    returned = lax.all_to_all(smoothed, "lat", split_axis=0, concat_axis=1, tiled=True)
    meridional = returned.reshape(lat_dev, lon_count, columns)
    zonal = zonal_rows(meridional, row_ids, all_rows)
    return control.astype(jnp.float32) + zonal


def solution(mesh):
    return jax.shard_map(
        local,
        mesh=mesh,
        in_specs=(
            P(("lat", "mem"), None),
            P(("lat", "mem"), None),
            P(("lat", "mem")),
            P(("lat", "mem")),
            P("lat", None, "mem"),
            P("lat", None, "mem"),
        ),
        out_specs=P("lat", None, "mem"),
        check_vma=False,
    )
```

profile of v0, /device:TPU:0, one launch (start us, length us, event | category | flops | bytes accessed | tf_op | source)
XLA Modules:
  0.0 131.8 jit_solution(14340743433858482917)
XLA Ops:
  6.5 0.7 fusion.41
  7.2 1.1 reduce-window.6
  8.4 0.2 slice_reduce_fusion
  8.6 0.8 fusion.34
  9.4 0.7 compare_select_fusion.2
  10.1 2.6 %scatter_custom_fusion = s32[512]{0:T(512)S(1)} fusion(s32[512]{0:T(512)S(1)} %bitcast.53, s32[512]{0:T(512)} %param.8, s32[]{:T(128)} %constant.94.clone.1), kind=kCustom, calls=%fused_computation.66 | custom fusion | bytes 2560 | tf_op jit(solution)/shard_map/scatter | solution.py:33
  12.7 0.7 all_to_all.11
  13.4 8.3 %all-to-all-start = ((s32[16,1,32]{2,1,0:T(1,128)}), s32[16,1,32]{2,1,0:T(1,128)S(1)}, u32[]{:S(2)}, u32[]{:S(2)}) async-start(s32[16,1,32]{2,1,0:T(1,128)} %all_to_all.11), calls=%async_computation | async-start | bytes 16384 | tf_op jit(solution)/shard_map/all_to_all | solution.py:74
  21.7 1.0 copy.14
  22.7 2.0 %scatter_custom_fusion.1 = f32[512,32]{1,0:T(8,128)S(1)} fusion(s32[512]{0:T(512)S(1)} %bitcast.54, f32[512,32]{1,0:T(8,128)S(1)} %copy.14, s32[512]{0:T(512)} %param.9, f32[]{:T(128)} %constant.93.clone.1), kind=kCustom, calls=%fused_computation.24 | custom fusion | flops 32768 | bytes 330752 | tf_op jit(solution)/shard_map/scatter | solution.py:31
  24.7 0.8 reshape.230
  25.5 3.5 %all-to-all-done = s32[16,1,32]{2,1,0:T(1,128)S(1)} async-done(((s32[16,1,32]{2,1,0:T(1,128)}), s32[16,1,32]{2,1,0:T(1,128)S(1)}, u32[]{:S(2)}, u32[]{:S(2)}) %all-to-all-start) | async-done | bytes 2080 | tf_op jit(solution)/shard_map/all_to_all | solution.py:74
  28.9 3.5 %all-to-all-start.1 = ((f32[16,1,1024]{2,1,0:T(1,128)}), f32[16,1,1024]{2,1,0:T(1,128)S(1)}, u32[]{:S(2)}, u32[]{:S(2)}) async-start(f32[16,1,1024]{2,1,0:T(1,128)} %reshape.230), calls=%async_computation.1 | async-start | bytes 131072 | tf_op jit(solution)/shard_map/all_to_all | solution.py:73
  32.5 0.0 all-reduce.2.cloned.1.call-start
  32.5 0.6 broadcast.218
  33.1 0.7 reduce.5
  33.8 0.1 reshape.185
  33.9 6.1 %all-to-all-done.1 = f32[16,1,1024]{2,1,0:T(1,128)S(1)} async-done(((f32[16,1,1024]{2,1,0:T(1,128)}), f32[16,1,1024]{2,1,0:T(1,128)S(1)}, u32[]{:S(2)}, u32[]{:S(2)}) %all-to-all-start.1) | async-done | bytes 65568 | tf_op jit(solution)/shard_map/all_to_all | solution.py:73
  40.0 0.5 broadcast.220
  40.5 0.8 reduce.6
  41.3 0.1 reshape.231
  41.4 0.0 copy-start
  41.4 3.1 %scatter_custom_fusion.2 = f32[1440,32]{1,0:T(8,128)} fusion(s32[512]{0:T(512)S(1)} %bitcast.55, f32[512,32]{1,0:T(8,128)S(1)} %bitcast.49, f32[]{:T(128)} %constant.93.clone.1), kind=kCustom, calls=%fused_computation.20 | custom fusion | flops 16384 | bytes 184324 | tf_op jit(solution)/shard_map/scatter-add | solution.py:45
  44.5 0.0 all-reduce.2.cloned.1.call-update
  44.5 0.0 copy-done
  44.5 0.2 copy.12
  44.7 15.8 %all-reduce.2.cloned.1.call-done = f32[1440,32]{1,0:T(8,128)} async-done(((f32[1440,32]{1,0:T(8,128)}), f32[1440,32]{1,0:T(8,128)}) %all-reduce.2.cloned.1.call-update) | async-done | bytes 184336 | tf_op jit(solution)/shard_map/psum | solution.py:77
  60.6 1.3 %copy.15 = f32[1440,32]{0,1:T(8,128)S(1)} copy(f32[1440,32]{1,0:T(8,128)} %all-reduce.2.cloned.1.call-done) | data formatting | bytes 368640 | tf_op jit(solution)/shard_map/psum | solution.py:77
  61.9 0.1 mul.54
  62.0 1.4 %fusion.15 = f32[1440,128]{1,0:T(8,128)S(1)} fusion(f32[1440,128]{0,1:T(8,128)S(1)} %bitcast.45, bf16[1,1440,128]{1,2,0:T(8,128)(2,1)S(1)} %copy.12, f32[128]{0:T(128)S(1)} %get-tuple-element.16, s32[128]{0:T(128)S(1)} %get-tuple-element.11), kind=kOutput, calls=%fused_computation.16 | convolution fusion | flops 283566080 | bytes 1844224 | tf_op jit(solution)/shard_map/dot_general | solution.py:90
  63.4 27.4 %all_to_all.32 = f32[1,16,11520]{2,0,1:T(1,128)S(1)} all-to-all(f32[1,16,11520]{2,0,1:T(1,128)S(1)} %bitcast.46), channel_id=1, replica_groups=mesh['lat'=16,'mem'=2] {'lat'}, dimensions={1} | all-to-all | bytes 1474560 | tf_op jit(solution)/shard_map/all_to_all | solution.py:99
  90.8 0.8 convolution_bitcast_fusion
  91.6 1.6 %copy.17 = f32[16,1,11520]{2,1,0:T(1,128)} copy(f32[16,1,11520]{2,0,1:T(8,128)S(1)} %convolution_bitcast_fusion) | data formatting | bytes 1474560 | tf_op jit(solution)/shard_map/rR,Rgc->rgc/dot_general | solution.py:96
  93.2 0.0 copy-start.1
  93.2 3.9 %all-to-all-start.3 = ((f32[16,1,11520]{2,1,0:T(1,128)}), f32[16,1,11520]{2,1,0:T(1,128)S(1)}, u32[]{:S(2)}, u32[]{:S(2)}) async-start(f32[16,1,11520]{2,1,0:T(1,128)} %copy.17), calls=%async_computation.3 | async-start | bytes 1474560 | tf_op jit(solution)/shard_map/all_to_all | solution.py:102
  97.2 17.5 %all-to-all-done.3 = f32[16,1,11520]{2,1,0:T(1,128)S(1)} async-done(((f32[16,1,11520]{2,1,0:T(1,128)}), f32[16,1,11520]{2,1,0:T(1,128)S(1)}, u32[]{:S(2)}, u32[]{:S(2)}) %all-to-all-start.3) | async-done | bytes 737312 | tf_op jit(solution)/shard_map/all_to_all | solution.py:102
  114.8 0.0 copy-done.1
  114.8 10.2 %fusion.12 = f32[1,1440,128]{2,1,0:T(8,128)} fusion(f32[1440,128]{1,0:T(8,128)S(1)} %bitcast.48, f32[]{:T(128)S(6)} %div.37, bf16[1,1440,128]{2,1,0:T(8,128)(2,1)S(1)} %copy-done.1), kind=kOutput, calls=%fused_computation.14 | convolution fusion | flops 3199933440 | bytes 1843204 | tf_op jit(solution)/shard_map/while/body/eval_jaxpr/dot_general | solution.py:56
  (4 shorter events, 0.1 us)
Async XLA Ops:
  13.4 15.6 %all-to-all-start = ((s32[16,1,32]{2,1,0:T(1,128)}), s32[16,1,32]{2,1,0:T(1,128)S(1)}, u32[]{:S(2)}, u32[]{:S(2)}) async-start(s32[16,1,32]{2,1,0:T(1,128)} %all_to_all.11), calls=%async_computation | async-start | bytes 16384 | tf_op jit(solution)/shard_map/all_to_all | solution.py:74
  28.9 11.0 %all-to-all-start.1 = ((f32[16,1,1024]{2,1,0:T(1,128)}), f32[16,1,1024]{2,1,0:T(1,128)S(1)}, u32[]{:S(2)}, u32[]{:S(2)}) async-start(f32[16,1,1024]{2,1,0:T(1,128)} %reshape.230), calls=%async_computation.1 | async-start | bytes 131072 | tf_op jit(solution)/shard_map/all_to_all | solution.py:73
  32.5 28.1 %all-reduce.2.cloned.1.call-start = ((), (), s32[]{:S(2)}) async-start(), calls=%async_computation.4 | async-start | bytes 1474560 | tf_op jit(solution)/shard_map/psum | solution.py:77
  41.4 3.1 %copy-start = (bf16[1,1440,128]{2,1,0:T(8,128)(2,1)S(1)}, bf16[1,1440,128]{2,1,0:T(8,128)(2,1)}, u32[]{:S(2)}) copy-start(bf16[1,1440,128]{2,1,0:T(8,128)(2,1)} %param.10) | copy-start | bytes 1105924
  93.2 21.6 %copy-start.1 = (bf16[1,1440,128]{2,1,0:T(8,128)(2,1)S(1)}, bf16[1,1440,128]{2,1,0:T(8,128)(2,1)}, u32[]{:S(2)}) copy-start(bf16[1,1440,128]{2,1,0:T(8,128)(2,1)} %param.11) | copy-start | bytes 1105924
  93.2 21.6 %all-to-all-start.3 = ((f32[16,1,11520]{2,1,0:T(1,128)}), f32[16,1,11520]{2,1,0:T(1,128)S(1)}, u32[]{:S(2)}, u32[]{:S(2)}) async-start(f32[16,1,11520]{2,1,0:T(1,128)} %copy.17), calls=%async_computation.3 | async-start | bytes 1474560 | tf_op jit(solution)/shard_map/all_to_all | solution.py:102
Sparse Core Ops, SparseCore 0:
  44.7 15.8 all-reduce.1
where the time goes:
time: 132 us
  waiting for transfers between devices  42.9 us (32%)
  blocking collectives  27.4 us (21%)
  starting transfers between devices  15.8 us (12%)
  between operations  13.6 us (10%)
  matrix products  12.4 us (9%)
  other arithmetic  9.99 us (8%)
  local copies, waits for them, and re-layouts  9.78 us (7%)
    all_to_all x1, blocking collectives, local(): lax.all_to_all(pieces, 'lat', split_axis=1, concat_axis=0, tiled=True)  27.4 us
    all_to_all x1, waiting for transfers between devices, local(): lax.all_to_all(smoothed, 'lat', split_axis=0, concat_axis=1, tiled=True)  17.5 us
    psum x1, waiting for transfers between devices, local(): innovation = lax.psum(partial_grid, 'mem')  15.8 us
    dot_general x1, matrix products, one_row(): jnp.dot(lonk, row_field, precision=lax.Precision.HIGHEST, preferred_eleme...  10.2 us
    all_to_all x1, starting transfers between devices, local(): lax.all_to_all(send_cells, 'lat', split_axis=0, concat_axis=0, tiled=True)  8.31 us
    all_to_all x1, waiting for transfers between devices, local(): lax.all_to_all(send_rows, 'lat', split_axis=0, concat_axis=0, tiled=True)  6.05 us
    all_to_all x1, starting transfers between devices, local(): lax.all_to_all(smoothed, 'lat', split_axis=0, concat_axis=1, tiled=True)  3.92 us
    all_to_all x1, starting transfers between devices, local(): lax.all_to_all(send_rows, 'lat', split_axis=0, concat_axis=0, tiled=True)  3.5 us
  transfers between devices with their start and end apart: 4, of which 4 were waited for; matrix products, arithmetic and copies ran while one was open for 4% of the time, Pallas kernels for 0%

commit v1 on v0

v1 whole, which is shorter than its diff:
```python
import functools
import math

import jax
import jax.numpy as jnp
import numpy as np
from jax import lax
from jax.experimental import pallas as pl
from jax.experimental.pallas import tpu as pltpu
from jax.sharding import PartitionSpec as P

CAP = 32
PARTS = 3
BLOCKS = 3
QUADS = 4
HIGHEST = lax.Precision.HIGHEST
F32 = jnp.float32
BF16 = jnp.bfloat16


def iota(shape, axis):
    return lax.broadcasted_iota(jnp.int32, shape, axis)


def split(value):
    high = value.astype(BF16)
    return high, (value - high.astype(F32)).astype(BF16)


def dot(left, right):
    return jnp.dot(left, right, preferred_element_type=F32)


def make_messages(me, meta_ref, rows_ref, msg_ref, n):
    count, levels = rows_ref.shape
    band_row = meta_ref[0:1, :]
    eye = iota((count, count), 0) == iota((count, count), 1)
    column = lambda row: jnp.sum(jnp.where(eye, row, 0.0), axis=1, keepdims=True)
    band_col, cell_col, top_col = (column(meta_ref[i : i + 1, :]) for i in range(3))
    same = band_row == band_col
    below = iota((count, count), 1) < iota((count, count), 0)
    above = iota((count, count), 1) > iota((count, count), 0)
    rank_col = jnp.sum(jnp.where(same & below, 1.0, 0.0), axis=1, keepdims=True)
    rank_row = jnp.sum(jnp.where(same & above, 1.0, 0.0), axis=0, keepdims=True)
    quad_col, quad_row = jnp.floor(rank_col * 0.125), jnp.floor(rank_row * 0.125)
    place_col, place_row = rank_col - 8.0 * quad_col, rank_row - 8.0 * quad_row
    slot = iota((n * 8, count), 0).astype(F32)
    lane = iota((count, 128), 1)
    wide = jnp.concatenate([rows_ref[...]] * QUADS, axis=1)
    keep = ((lane // levels).astype(F32) == quad_col) & ((lane % levels).astype(F32) < top_col)
    values = jnp.dot(
        jnp.where(band_row * 8.0 + place_row == slot, 1.0, 0.0),
        jnp.where(keep, wide, 0.0),
        precision=HIGHEST,
        preferred_element_type=F32,
    )
    mine = lax.rem(me * 8, 128)
    cells = jnp.dot(
        jnp.where(band_row * 8.0 + quad_row == slot, 1.0, 0.0),
        jnp.where((lane - mine).astype(F32) == place_col, cell_col, 0.0),
        precision=HIGHEST,
        preferred_element_type=F32,
    )
    msg_ref[:, 0:8, :] = values.reshape(n, 8, 128)
    msg_ref[:, 8:16, :] = cells.reshape(n, 8, 128)


def body(
    n, mems, owners, part_rows,
    meta_ref, rows_ref, perturb_ref, control_ref,
    out_ref,
    msg_ref, obs_ref, rhs_ref, cells_ref, inno_ref, v_ref, got_ref, m_ref, back_ref, g_hi, g_lo,
    obs_send, obs_recv, mem_send, mem_recv, v_send, v_recv, m_send, m_recv,
):
    me, mem = lax.axis_index("lat"), lax.axis_index("mem")
    lon, columns = out_ref.shape[1:]
    levels = rows_ref.shape[1]
    chunk = PARTS * part_rows

    barrier = pltpu.get_barrier_semaphore()

    def greet(k, carry):
        pl.semaphore_signal(barrier, inc=1, device_id={"lat": lax.rem(me + k, n)})
        return carry

    lax.fori_loop(1, n, greet, 0)
    for k in range(1, mems):
        pl.semaphore_signal(barrier, inc=1, device_id={"mem": lax.rem(mem + k, mems)})
    make_messages(me, meta_ref, rows_ref, msg_ref, n)
    pl.semaphore_wait(barrier, n - 1 + mems - 1)

    def obs_copy(k):
        there = lax.rem(me + k, n)
        return pltpu.make_async_remote_copy(
            src_ref=msg_ref.at[there], dst_ref=obs_ref.at[mem, me],
            send_sem=obs_send.at[k], recv_sem=obs_recv, device_id={"lat": there},
        )

    def start_obs(k, carry):
        obs_copy(k).start()
        return carry

    lax.fori_loop(1, n, start_obs, 0)
    obs_ref[mem, me] = msg_ref[me]
    local = obs_ref.at[mem, pl.ds(0, n - 1)]
    pltpu.make_async_copy(local, local, obs_recv).wait()

    def mem_copy(k):
        return pltpu.make_async_remote_copy(
            src_ref=obs_ref.at[mem], dst_ref=obs_ref.at[mem],
            send_sem=mem_send.at[k], recv_sem=mem_recv.at[k],
            device_id={"mem": lax.rem(mem + k, mems)},
        )

    for k in range(1, mems):
        mem_copy(k).start()
    for k in range(1, mems):
        mem_copy(k).wait()

    groups = n // 16
    group_slots = 128 * QUADS
    depth = mems * groups

    def stage(i, carry):
        m, t = i // groups, lax.rem(i, groups)
        source = pl.ds(t * 16, 16)
        rows = obs_ref[m, source, 0:8, :].reshape(128, 128)
        cells_ref[i] = jnp.sum(obs_ref[m, source, 8:16, :], axis=0)
        for q in range(QUADS):
            tiled = jnp.concatenate([rows[:, q * levels : (q + 1) * levels]] * QUADS, axis=1)
            high, low = split(tiled)
            rhs_ref[i, q * 128 : (q + 1) * 128, 0:128] = high
            rhs_ref[i, q * 128 : (q + 1) * 128, 128:256] = low
        return carry

    lax.fori_loop(0, depth, stage, 0)

    a, b = iota((columns, columns), 0), iota((columns, columns), 1)
    gap = (a % levels - b % levels).astype(F32)
    vert = jnp.where(a // levels == b // levels, jnp.exp(-0.5 * gap * gap), 0.0)
    vert_hi, vert_lo = split(vert)
    vert_both = jnp.concatenate([vert_hi, vert_hi], axis=0)

    block_rows = lon // BLOCKS
    block_owners = owners // BLOCKS

    def v_copy(dest, p):
        return pltpu.make_async_remote_copy(
            src_ref=v_ref.at[dest * PARTS + p], dst_ref=got_ref.at[p, me],
            send_sem=v_send.at[p, dest], recv_sem=v_recv.at[p], device_id={"lat": dest},
        )

    def send_block(block, p):
        def one(k, carry):
            dest = block * block_owners + lax.rem(me + k, block_owners)

            @pl.when(dest != me)
            def _():
                v_copy(dest, p).start()

            return carry

        lax.fori_loop(0, block_owners, one, 0)

    first = (me * BLOCKS) // n
    for step in range(BLOCKS):
        block = lax.rem(first + step, BLOCKS)
        base = block * block_rows
        position = (iota((block_rows, 128), 0) + base).astype(F32)

        def deposit(i):
            cells = cells_ref[i]
            hot = jnp.concatenate(
                [
                    jnp.where(position == cells[q : q + 1, :], 1.0, 0.0).astype(BF16)
                    for q in range(QUADS)
                ],
                axis=1,
            )
            return dot(hot, rhs_ref[i])

        inno_ref[...] = deposit(0)

        def more(i, carry):
            inno_ref[...] += deposit(i)
            return carry

        lax.fori_loop(1, depth, more, 0)
        innovation = inno_ref[:, 0:128] + inno_ref[:, 128:256]
        field = perturb_ref[0, pl.ds(pl.multiple_of(base, 16), block_rows), :].astype(F32)
        high, low = split(field * innovation)
        vertical = dot(jnp.concatenate([high, low], axis=1), vert_both) + dot(high, vert_lo)
        v_ref[pl.ds(block * (block_rows // part_rows), block_rows // part_rows)] = (
            vertical.reshape(block_rows // part_rows, part_rows, columns)
        )
        send_block(block, 0)
    for p in range(1, PARTS):
        for step in range(BLOCKS):
            send_block(lax.rem(first + step, BLOCKS), p)

    @pl.when(me < owners)
    def _():
        for p in range(PARTS):
            got_ref[p, me] = v_ref[me * PARTS + p]

    half = owners * part_rows
    spread = max(lon // 60, 4) / jnp.cos(
        1.2 * (jnp.full((1, half), me, jnp.int32).astype(F32) + 0.5) / n
    )
    scale = 1.0 / spread
    tile = 48

    def zonal_kernel(i, carry):
        start = pl.multiple_of(i * tile, tile)
        row = iota((tile, half), 0) + start
        for p in range(PARTS):
            k = iota((1, half), 1)
            col = (k // part_rows) * chunk + p * part_rows + k % part_rows
            distance = jnp.abs(row - col).astype(F32)
            distance = jnp.minimum(distance, lon - distance)
            ratio = distance * scale
            high, low = split(jnp.exp(-0.5 * (ratio * ratio)))
            g_hi[p, pl.ds(start, tile), :] = high
            g_lo[p, pl.ds(start, tile), :] = low
        return carry

    lax.fori_loop(0, lon // tile, zonal_kernel, 0)

    weights = [float(np.exp(np.float32(-0.5) * np.float32(d / 8.0) ** 2)) for d in range(n)]

    def m_copy(k, p):
        dest = lax.rem(me + k, n)
        return pltpu.make_async_remote_copy(
            src_ref=m_ref.at[p, dest], dst_ref=back_ref.at[p, me],
            send_sem=m_send.at[p, k], recv_sem=m_recv.at[p], device_id={"lat": dest},
        )

    @pl.when(me < owners)
    def _():
        for p in range(PARTS):
            arrived = got_ref.at[p, pl.ds(0, n - 1)]
            pltpu.make_async_copy(arrived, arrived, v_recv.at[p]).wait()

            def smooth(i, carry):
                rows = pl.ds(pl.multiple_of(i * 8, 8), 8)
                fields = [got_ref[p, r, rows, :] for r in range(n)]
                for r in range(n):
                    terms = [weights[abs(r - s)] * fields[s] for s in range(n)]
                    while len(terms) > 1:
                        terms = [terms[j] + terms[j + 1] for j in range(0, len(terms), 2)]
                    m_ref[p, r, rows, :] = terms[0]
                return carry

            lax.fori_loop(0, part_rows // 8, smooth, 0)

            def start_m(k, carry):
                m_copy(k, p).start()
                return carry

            lax.fori_loop(1, n, start_m, 0)
            back_ref[p, me] = m_ref[p, me]

    out_ref[0] = control_ref[0].astype(F32)
    for p in range(PARTS):
        for own, total in ((True, owners - 1), (False, owners)):

            @pl.when((me < owners) == own)
            def _():
                arrived = back_ref.at[p, pl.ds(0, total)]
                pltpu.make_async_copy(arrived, arrived, m_recv.at[p]).wait()

        high, low = split(back_ref[p].reshape(half, columns))
        both = jnp.concatenate([high, low], axis=1)
        for step in range(BLOCKS):
            rows = pl.ds(step * block_rows, block_rows)
            wide = dot(g_hi[p, rows, :], both)
            narrow = dot(g_lo[p, rows, :], high)
            out_ref[0, rows, :] += wide[:, 0:128] + (wide[:, 128:256] + narrow)

    def end_obs(k, carry):
        obs_copy(k).wait_send()
        return carry

    lax.fori_loop(1, n, end_obs, 0)
    for p in range(PARTS):

        def end_v(dest, carry):
            @pl.when(dest != me)
            def _():
                v_copy(dest, p).wait_send()

            return carry

        lax.fori_loop(0, owners, end_v, 0)

    @pl.when(me < owners)
    def _():
        for p in range(PARTS):

            def end_m(k, carry):
                m_copy(k, p).wait_send()
                return carry

            lax.fori_loop(1, n, end_m, 0)


def local(n, mems, obs_rows, obs_band, obs_cell, obs_top, perturb, control):
    _, lon, columns = perturb.shape
    count, levels = obs_rows.shape
    chunk = -(-lon // (n * 8 * PARTS)) * 8 * PARTS
    owners, part_rows = lon // chunk, chunk // PARTS
    assert owners * chunk == lon and owners % BLOCKS == 0 and owners <= n
    half = owners * part_rows
    depth = mems * n // 16
    meta = jnp.stack([obs_band.reshape(count), obs_cell, obs_top]).astype(F32)
    dma = pltpu.SemaphoreType.DMA
    return pl.pallas_call(
        functools.partial(body, n, mems, owners, part_rows),
        out_shape=jax.ShapeDtypeStruct((1, lon, columns), F32),
        in_specs=[pl.BlockSpec(memory_space=pltpu.VMEM)] * 4,
        out_specs=pl.BlockSpec(memory_space=pltpu.VMEM),
        scratch_shapes=[
            pltpu.VMEM((n, 16, 128), F32),
            pltpu.VMEM((mems, n, 16, 128), F32),
            pltpu.VMEM((depth, 128 * QUADS, 256), BF16),
            pltpu.VMEM((depth, 8, 128), F32),
            pltpu.VMEM((lon // BLOCKS, 256), F32),
            pltpu.VMEM((owners * PARTS, part_rows, columns), F32),
            pltpu.VMEM((PARTS, n, part_rows, columns), F32),
            pltpu.VMEM((PARTS, n, part_rows, columns), F32),
            pltpu.VMEM((PARTS, owners, part_rows, columns), F32),
            pltpu.VMEM((PARTS, lon, half), BF16),
            pltpu.VMEM((PARTS, lon, half), BF16),
            dma((n,)), dma(()), dma((mems,)), dma((mems,)),
            dma((PARTS, n)), dma((PARTS,)), dma((PARTS, n)), dma((PARTS,)),
        ],
        compiler_params=pltpu.CompilerParams(
            collective_id=0, has_side_effects=True, vmem_limit_bytes=56 * 1024 * 1024
        ),
    )(meta, obs_rows, perturb, control)


def solution(mesh):
    return jax.shard_map(
        functools.partial(local, mesh.shape["lat"], mesh.shape["mem"]),
        mesh=mesh,
        in_specs=(
            P(("lat", "mem"), None),
            P(("lat", "mem"), None),
            P(("lat", "mem")),
            P(("lat", "mem")),
            P("lat", None, "mem"),
            P("lat", None, "mem"),
        ),
        out_specs=P("lat", None, "mem"),
        check_vma=False,
    )
```

time: 132 us -> 59.6 us (0.45)
  Pallas kernels: 0 us -> 53.6 us
  waiting for transfers between devices: 42.9 us -> 0 us
  blocking collectives: 27.4 us -> 0 us
  starting transfers between devices: 15.8 us -> 0 us
  between operations: 13.6 us -> 0.01 us
  matrix products: 12.4 us -> 0 us
  other arithmetic: 9.99 us -> 1.29 us
  local copies, waits for them, and re-layouts: 9.78 us -> 4.4 us
    pallas_call x0 -> x1, Pallas kernels: none -> 53.6 us  [local(): pl.pallas_call(functools.partial(body, n, mems, owners, part_rows), out_s...]
    all_to_all x1 -> x0, blocking collectives: 27.4 us -> none  [local(): lax.all_to_all(pieces, 'lat', split_axis=1, concat_axis=0, tiled=True)]
    all_to_all x3 -> x0, waiting for transfers between devices: 27 us -> none  [the longest x1 17.5 us: local(): lax.all_to_all(smoothed, 'lat', split_axis=0, concat_axis=1, tiled=True)]
    psum x1 -> x0, waiting for transfers between devices: 15.8 us -> none  [local(): innovation = lax.psum(partial_grid, 'mem')]
    all_to_all x3 -> x0, starting transfers between devices: 15.7 us -> none  [the longest x1 8.31 us: local(): lax.all_to_all(send_cells, 'lat', split_axis=0, concat_axis=0, tiled=True)]
    dot_general x3 -> x0, matrix products: 12.4 us -> none  [the longest x1 10.2 us: one_row(): jnp.dot(lonk, row_field, precision=lax.Precision.HIGHEST, preferred_eleme...]
    scatter-add x1 -> x0, other arithmetic: 3.11 us -> none  [deposit(): jnp.zeros((band_cells, levels), jnp.float32).at[target_cell].add(flat_rows)]
    scatter x1 -> x0, local copies, waits for them, and re-layouts: 2.59 us -> none  [bucket(): jnp.full((band_count * capacity,), -1, jnp.int32).at[target_slot]]
  transfers between devices with their start and end apart: 4 -> 0, of which waited for: 4 -> 0; matrix products, arithmetic and copies ran while one was open for 4% -> 0% of each run, Pallas kernels for 0% -> 0%
where the time goes in v1:
time: 59.6 us; the launch traced here: 59.3 us
  Pallas kernels  53.6 us (90%)
  local copies, waits for them, and re-layouts  4.4 us (7%)
  other arithmetic  1.29 us (2%)
    pallas_call x1, Pallas kernels, local(): pl.pallas_call(functools.partial(body, n, mems, owners, part_rows), out_s...  53.6 us
    unnamed x6, local copies, waits for them, and re-layouts  4.4 us
    convert_element_type x1, other arithmetic, local(): meta = jnp.stack([obs_band.reshape(count), obs_cell, obs_top]).astype(F32)  1.29 us

profile of v1, /device:TPU:0, one launch (start us, length us, event | category | flops | bytes accessed | tf_op | source)
XLA Modules:
  0.0 59.3 jit_solution(13980856200231834202)
XLA Ops:
  0.0 0.0 copy-start.1
  0.0 0.0 copy-start
  0.0 0.7 %copy-done.1 = s32[512]{0:T(512)S(1)} copy-done((s32[512]{0:T(512)S(1)}, s32[512]{0:T(512)}, u32[]{:S(2)}) %copy-start.1) | copy-done | bytes 2072
  0.7 0.0 copy-done
  0.7 1.3 %add_convert_fusion.meta_ref = f32[3,512]{1,0:T(4,128)} fusion(s32[1,512]{1,0:T(1,128)S(1)} %bitcast.3, s32[1,512]{1,0:T(1,128)S(1)} %bitcast.4, s32[1,512]{1,0:T(1,128)} %bitcast.5), kind=kLoop, calls=%fused_computation | loop fusion | flops 4608 | bytes 12288 | tf_op jit(solution)/shard_map/convert_element_type | solution.py:315
  2.0 1.7 %copy.7.rows_ref = f32[512,32]{1,0:T(8,128)} copy(f32[512,32]{0,1:T(8,128)} %param.6) | data formatting | bytes 131072 | tf_op args[0]
  3.7 53.6 %shard_map.64 = f32[1,1440,128]{2,1,0:T(8,128)} custom-call(f32[3,512]{1,0:T(4,128)} %add_convert_fusion.meta_ref, f32[512,32]{1,0:T(8,128)} %copy.7.rows_ref, bf16[1,1440,128]{2,1,0:T(8,128)(2,1)} %perturb_ref.1, bf16[1,1440,128]{2,1,0:T(8,128)(2,1)} %control_ref.1), custom_call_target="tpu_custom_call" | custom-call | tf_op jit(solution)/shard_map/pallas_call | solution.py:317
  57.3 2.0 %copy.9 = f32[1,1440,128]{2,1,0:T(8,128)} copy(f32[1,1440,128]{2,1,0:T(8,128)} %shard_map.64) | data formatting | bytes 1474560
Async XLA Ops:
  0.0 0.7 %copy-start.1 = (s32[512]{0:T(512)S(1)}, s32[512]{0:T(512)}, u32[]{:S(2)}) copy-start(s32[512]{0:T(512)} %param.8) | copy-start | bytes 6148
  0.0 0.7 %copy-start = (s32[512]{0:T(512)S(1)}, s32[512]{0:T(512)}, u32[]{:S(2)}) copy-start(s32[512]{0:T(512)} %param.9) | copy-start | bytes 6148

commit v2 on v1

--- a/solution.py
+++ b/solution.py
@@ -13,7 +13,6 @@
 PARTS = 3
 BLOCKS = 3
 QUADS = 4
-HIGHEST = lax.Precision.HIGHEST
 F32 = jnp.float32
 BF16 = jnp.bfloat16
 
@@ -31,50 +30,49 @@
     return jnp.dot(left, right, preferred_element_type=F32)
 
 
-def make_messages(me, meta_ref, rows_ref, msg_ref, n):
-    count, levels = rows_ref.shape
-    band_row = meta_ref[0:1, :]
-    eye = iota((count, count), 0) == iota((count, count), 1)
-    column = lambda row: jnp.sum(jnp.where(eye, row, 0.0), axis=1, keepdims=True)
-    band_col, cell_col, top_col = (column(meta_ref[i : i + 1, :]) for i in range(3))
-    same = band_row == band_col
-    below = iota((count, count), 1) < iota((count, count), 0)
-    above = iota((count, count), 1) > iota((count, count), 0)
-    rank_col = jnp.sum(jnp.where(same & below, 1.0, 0.0), axis=1, keepdims=True)
-    rank_row = jnp.sum(jnp.where(same & above, 1.0, 0.0), axis=0, keepdims=True)
-    quad_col, quad_row = jnp.floor(rank_col * 0.125), jnp.floor(rank_row * 0.125)
-    place_col, place_row = rank_col - 8.0 * quad_col, rank_row - 8.0 * quad_row
-    slot = iota((n * 8, count), 0).astype(F32)
-    lane = iota((count, 128), 1)
-    wide = jnp.concatenate([rows_ref[...]] * QUADS, axis=1)
-    keep = ((lane // levels).astype(F32) == quad_col) & ((lane % levels).astype(F32) < top_col)
-    values = jnp.dot(
-        jnp.where(band_row * 8.0 + place_row == slot, 1.0, 0.0),
-        jnp.where(keep, wide, 0.0),
-        precision=HIGHEST,
-        preferred_element_type=F32,
+def dot_nt(left, right):
+    return lax.dot_general(left, right, (((1,), (1,)), ((), ())), preferred_element_type=F32)
+
+
+def make_messages(me, rows_ref, band_ref, cell_ref, top_ref, msg_ref, n):
+    levels, count = rows_ref.shape
+    band = band_ref[...]
+    named = iota((n, count), 0) == band
+    before = iota((count, count), 0) < iota((count, count), 1)
+    earlier = dot(
+        jnp.where(named, 1.0, 0.0).astype(BF16), jnp.where(before, 1.0, 0.0).astype(BF16)
+    )
+    rank = jnp.sum(jnp.where(named, earlier, 0.0), axis=0, keepdims=True).astype(jnp.int32)
+    quad, place = rank // 8, rank % 8
+    slot = iota((n * 8, count), 0)
+    line = iota((128, count), 0)
+    wide = jnp.concatenate([rows_ref[...]] * QUADS, axis=0)
+    keep = (line // levels == quad) & (line % levels < top_ref[...])
+    high, low = split(jnp.where(keep, wide, 0.0))
+    values = dot_nt(
+        jnp.where(band * 8 + place == slot, 1.0, 0.0).astype(BF16),
+        jnp.concatenate([high, low], axis=0),
     )
     mine = lax.rem(me * 8, 128)
-    cells = jnp.dot(
-        jnp.where(band_row * 8.0 + quad_row == slot, 1.0, 0.0),
-        jnp.where((lane - mine).astype(F32) == place_col, cell_col, 0.0),
-        precision=HIGHEST,
-        preferred_element_type=F32,
-    )
-    msg_ref[:, 0:8, :] = values.reshape(n, 8, 128)
-    msg_ref[:, 8:16, :] = cells.reshape(n, 8, 128)
+    high, low = split(jnp.where(line - mine == place, cell_ref[...].astype(F32), 0.0))
+    cells = dot_nt(
+        jnp.where(band * 8 + quad == slot, 1.0, 0.0).astype(BF16),
+        jnp.concatenate([high, low], axis=0),
+    )
+    msg_ref[:, 0:8, :] = (values[:, 0:128] + values[:, 128:256]).reshape(n, 8, 128)
+    msg_ref[:, 8:16, :] = (cells[:, 0:128] + cells[:, 128:256]).reshape(n, 8, 128)
 
 
 def body(
     n, mems, owners, part_rows,
-    meta_ref, rows_ref, perturb_ref, control_ref,
+    rows_ref, band_ref, cell_ref, top_ref, perturb_ref,
     out_ref,
     msg_ref, obs_ref, rhs_ref, cells_ref, inno_ref, v_ref, got_ref, m_ref, back_ref, g_hi, g_lo,
     obs_send, obs_recv, mem_send, mem_recv, v_send, v_recv, m_send, m_recv,
 ):
     me, mem = lax.axis_index("lat"), lax.axis_index("mem")
     lon, columns = out_ref.shape[1:]
-    levels = rows_ref.shape[1]
+    levels = rows_ref.shape[0]
     chunk = PARTS * part_rows
 
     barrier = pltpu.get_barrier_semaphore()
@@ -86,7 +84,7 @@
     lax.fori_loop(1, n, greet, 0)
     for k in range(1, mems):
         pl.semaphore_signal(barrier, inc=1, device_id={"mem": lax.rem(mem + k, mems)})
-    make_messages(me, meta_ref, rows_ref, msg_ref, n)
+    make_messages(me, rows_ref, band_ref, cell_ref, top_ref, msg_ref, n)
     pl.semaphore_wait(barrier, n - 1 + mems - 1)
 
     def obs_copy(k):
@@ -102,6 +100,36 @@
 
     lax.fori_loop(1, n, start_obs, 0)
     obs_ref[mem, me] = msg_ref[me]
+
+    half = owners * part_rows
+    tile = 48
+
+    def zonal_kernel(p):
+        spread = max(lon // 60, 4) / jnp.cos(
+            1.2 * (jnp.full((1, half), me, jnp.int32).astype(F32) + 0.5) / n
+        )
+        scale = 1.0 / spread
+        k = iota((1, half), 1)
+        col = (k // part_rows) * chunk + p * part_rows + k % part_rows
+
+        def rows_of(i, carry):
+            start = pl.multiple_of(i * tile, tile)
+            distance = jnp.abs(iota((tile, half), 0) + start - col).astype(F32)
+            ratio = jnp.minimum(distance, lon - distance) * scale
+            high, low = split(jnp.exp(-0.5 * (ratio * ratio)))
+            g_hi[p, pl.ds(start, tile), :] = high
+            g_lo[p, pl.ds(start, tile), :] = low
+            return carry
+
+        lax.fori_loop(0, lon // tile, rows_of, 0)
+
+    zonal_kernel(0)
+    a, b = iota((columns, columns), 0), iota((columns, columns), 1)
+    gap = (a % levels - b % levels).astype(F32)
+    vert = jnp.where(a // levels == b // levels, jnp.exp(-0.5 * gap * gap), 0.0)
+    vert_hi, vert_lo = split(vert)
+    vert_both = jnp.concatenate([vert_hi, vert_hi], axis=0)
+
     local = obs_ref.at[mem, pl.ds(0, n - 1)]
     pltpu.make_async_copy(local, local, obs_recv).wait()
 
@@ -135,12 +163,6 @@
 
     lax.fori_loop(0, depth, stage, 0)
 
-    a, b = iota((columns, columns), 0), iota((columns, columns), 1)
-    gap = (a % levels - b % levels).astype(F32)
-    vert = jnp.where(a // levels == b // levels, jnp.exp(-0.5 * gap * gap), 0.0)
-    vert_hi, vert_lo = split(vert)
-    vert_both = jnp.concatenate([vert_hi, vert_hi], axis=0)
-
     block_rows = lon // BLOCKS
     block_owners = owners // BLOCKS
 
@@ -162,9 +184,15 @@
 
         lax.fori_loop(0, block_owners, one, 0)
 
-    first = (me * BLOCKS) // n
+    mid = n // 2
+    lower = me < mid
+
+    def order(k):
+        low_half = lower == (k >= mid)
+        return jnp.where(low_half, 0, mid) + lax.rem(me + k, mid)
+
     for step in range(BLOCKS):
-        block = lax.rem(first + step, BLOCKS)
+        block = jnp.where(lower, BLOCKS - 1 - step, step)
         base = block * block_rows
         position = (iota((block_rows, 128), 0) + base).astype(F32)
 
@@ -195,41 +223,31 @@
         )
         send_block(block, 0)
     for p in range(1, PARTS):
-        for step in range(BLOCKS):
-            send_block(lax.rem(first + step, BLOCKS), p)
+
+
+        def send_part(k, carry):
+            dest = order(k)
+
+            @pl.when((dest != me) & (dest < owners))
+            def _():
+                v_copy(dest, p).start()
+
+            return carry
+
+        lax.fori_loop(0, n, send_part, 0)
 
     @pl.when(me < owners)
     def _():
         for p in range(PARTS):
             got_ref[p, me] = v_ref[me * PARTS + p]
 
-    half = owners * part_rows
-    spread = max(lon // 60, 4) / jnp.cos(
-        1.2 * (jnp.full((1, half), me, jnp.int32).astype(F32) + 0.5) / n
-    )
-    scale = 1.0 / spread
-    tile = 48
-
-    def zonal_kernel(i, carry):
-        start = pl.multiple_of(i * tile, tile)
-        row = iota((tile, half), 0) + start
-        for p in range(PARTS):
-            k = iota((1, half), 1)
-            col = (k // part_rows) * chunk + p * part_rows + k % part_rows
-            distance = jnp.abs(row - col).astype(F32)
-            distance = jnp.minimum(distance, lon - distance)
-            ratio = distance * scale
-            high, low = split(jnp.exp(-0.5 * (ratio * ratio)))
-            g_hi[p, pl.ds(start, tile), :] = high
-            g_lo[p, pl.ds(start, tile), :] = low
-        return carry
-
-    lax.fori_loop(0, lon // tile, zonal_kernel, 0)
+    for p in range(1, PARTS):
+        zonal_kernel(p)
 
     weights = [float(np.exp(np.float32(-0.5) * np.float32(d / 8.0) ** 2)) for d in range(n)]
 
     def m_copy(k, p):
-        dest = lax.rem(me + k, n)
+        dest = order(k)
         return pltpu.make_async_remote_copy(
             src_ref=m_ref.at[p, dest], dst_ref=back_ref.at[p, me],
             send_sem=m_send.at[p, k], recv_sem=m_recv.at[p], device_id={"lat": dest},
@@ -257,10 +275,10 @@
                 m_copy(k, p).start()
                 return carry
 
-            lax.fori_loop(1, n, start_m, 0)
+            lax.fori_loop(0, mid, start_m, 0)
+            lax.fori_loop(mid + 1, n, start_m, 0)
             back_ref[p, me] = m_ref[p, me]
 
-    out_ref[0] = control_ref[0].astype(F32)
     for p in range(PARTS):
         for own, total in ((True, owners - 1), (False, owners)):
 
@@ -275,7 +293,8 @@
             rows = pl.ds(step * block_rows, block_rows)
             wide = dot(g_hi[p, rows, :], both)
             narrow = dot(g_lo[p, rows, :], high)
-            out_ref[0, rows, :] += wide[:, 0:128] + (wide[:, 128:256] + narrow)
+            total = wide[:, 0:128] + (wide[:, 128:256] + narrow)
+            out_ref[0, rows, :] = total if p == 0 else out_ref[0, rows, :] + total
 
     def end_obs(k, carry):
         obs_copy(k).wait_send()
@@ -301,7 +320,8 @@
                 m_copy(k, p).wait_send()
                 return carry
 
-            lax.fori_loop(1, n, end_m, 0)
+            lax.fori_loop(0, mid, end_m, 0)
+            lax.fori_loop(mid + 1, n, end_m, 0)
 
 
 def local(n, mems, obs_rows, obs_band, obs_cell, obs_top, perturb, control):
@@ -312,12 +332,11 @@
     assert owners * chunk == lon and owners % BLOCKS == 0 and owners <= n
     half = owners * part_rows
     depth = mems * n // 16
-    meta = jnp.stack([obs_band.reshape(count), obs_cell, obs_top]).astype(F32)
     dma = pltpu.SemaphoreType.DMA
-    return pl.pallas_call(
+    zonal = pl.pallas_call(
         functools.partial(body, n, mems, owners, part_rows),
         out_shape=jax.ShapeDtypeStruct((1, lon, columns), F32),
-        in_specs=[pl.BlockSpec(memory_space=pltpu.VMEM)] * 4,
+        in_specs=[pl.BlockSpec(memory_space=pltpu.VMEM)] * 5,
         out_specs=pl.BlockSpec(memory_space=pltpu.VMEM),
         scratch_shapes=[
             pltpu.VMEM((n, 16, 128), F32),
@@ -335,9 +354,13 @@
             dma((PARTS, n)), dma((PARTS,)), dma((PARTS, n)), dma((PARTS,)),
         ],
         compiler_params=pltpu.CompilerParams(
-            collective_id=0, has_side_effects=True, vmem_limit_bytes=56 * 1024 * 1024
+            collective_id=0, has_side_effects=True, vmem_limit_bytes=30 * 1024 * 1024
         ),
-    )(meta, obs_rows, perturb, control)
+    )(
+        obs_rows.T, obs_band.reshape(1, count), obs_cell.reshape(1, count),
+        obs_top.reshape(1, count), perturb,
+    )
+    return control.astype(F32) + zonal
 
 
 def solution(mesh):

time: 59.6 us -> 56.4 us (0.946)
  local copies, waits for them, and re-layouts: 4.4 us -> 2.54 us
  Pallas kernels: 53.6 us -> 52.7 us
    unnamed x6 -> x12, local copies, waits for them, and re-layouts: 4.4 us -> 2.54 us
    convert_element_type x1 -> x0, other arithmetic: 1.29 us -> none  [local(): meta = jnp.stack([obs_band.reshape(count), obs_cell, obs_top]).astype(F32)]
    add x0 -> x1, other arithmetic: none -> 0.93 us  [local(): return control.astype(F32) + zonal]
    pallas_call x1, Pallas kernels: 53.6 us -> 52.7 us  [local(): pl.pallas_call(functools.partial(body, n, mems, owners, part_rows), out_s...]
where the time goes in v2:
time: 56.4 us; the launch traced here: 56.2 us
  Pallas kernels  52.7 us (93%)
  local copies, waits for them, and re-layouts  2.54 us (5%)
  other arithmetic  0.93 us (2%)
    pallas_call x1, Pallas kernels, local(): pl.pallas_call(functools.partial(body, n, mems, owners, part_rows), out_s...  52.7 us
    unnamed x12, local copies, waits for them, and re-layouts  2.54 us

profile of v2, /device:TPU:0, one launch (start us, length us, event | category | flops | bytes accessed | tf_op | source)
XLA Modules:
  0.0 56.2 jit_solution(13324936752253480872)
XLA Ops:
  0.0 0.0 copy-start.4
  0.0 0.0 copy-start.3
  0.0 0.0 copy-start.2
  0.0 0.7 %copy-done.4 = s32[512]{0:T(512)S(1)} copy-done((s32[512]{0:T(512)S(1)}, s32[512]{0:T(512)}, u32[]{:S(2)}) %copy-start.4) | copy-done | bytes 2072
  0.7 0.0 copy-done.3
  0.7 0.0 copy-done.2
  0.7 0.0 copy-start
  0.7 1.0 %copy-done = bf16[1,1440,128]{2,1,0:T(8,128)(2,1)S(1)} copy-done((bf16[1,1440,128]{2,1,0:T(8,128)(2,1)S(1)}, bf16[1,1440,128]{2,1,0:T(8,128)(2,1)}, u32[]{:S(2)}) %copy-start) | copy-done | bytes 368664
  1.7 0.0 copy-start.1
  1.7 0.8 %copy-done.1 = f32[512,32]{0,1:T(8,128)S(1)} copy-done((f32[512,32]{0,1:T(8,128)S(1)}, f32[512,32]{0,1:T(8,128)}, u32[]{:S(2)}) %copy-start.1) | copy-done | bytes 65560
  2.5 0.0 copy-start.5
  2.5 52.7 %shard_map.64 = f32[1,1440,128]{2,1,0:T(8,128)S(1)} custom-call(f32[32,512]{1,0:T(8,128)S(1)} %bitcast.4, s32[1,512]{1,0:T(1,128)S(1)} %bitcast.5, s32[1,512]{1,0:T(1,128)S(1)} %bitcast.6, s32[1,512]{1,0:T(1,128)S(1)} %bitcast.7, bf16[1,1440,128]{2,1,0:T(8,128)(2,1)S(1)} %copy-done), custom_call_target="tpu_custom_call" | custom-call | tf_op jit(solution)/shard_map/pallas_call | solution.py:336
  55.3 0.0 copy-done.5
  55.3 0.9 %convert_add_fusion = f32[1,1440,128]{2,1,0:T(8,128)} fusion(f32[1,1440,128]{2,1,0:T(8,128)S(1)} %shard_map.64, bf16[1,1440,128]{2,1,0:T(8,128)(2,1)S(1)} %copy-done.5), kind=kLoop, calls=%fused_computation | loop fusion | flops 368640 | bytes 1843200 | tf_op jit(solution)/shard_map/add | solution.py:363
Async XLA Ops:
  0.0 0.7 %copy-start.4 = (s32[512]{0:T(512)S(1)}, s32[512]{0:T(512)}, u32[]{:S(2)}) copy-start(s32[512]{0:T(512)} %param.9) | copy-start | bytes 6148
  0.0 0.7 %copy-start.3 = (s32[512]{0:T(512)S(1)}, s32[512]{0:T(512)}, u32[]{:S(2)}) copy-start(s32[512]{0:T(512)} %param.8) | copy-start | bytes 6148
  0.0 0.7 %copy-start.2 = (s32[512,1]{0,1:T(1,128)S(1)}, s32[512,1]{0,1:T(1,128)}, u32[]{:S(2)}) copy-start(s32[512,1]{0,1:T(1,128)} %param.7) | copy-start | bytes 6148
  0.7 1.0 %copy-start = (bf16[1,1440,128]{2,1,0:T(8,128)(2,1)S(1)}, bf16[1,1440,128]{2,1,0:T(8,128)(2,1)}, u32[]{:S(2)}) copy-start(bf16[1,1440,128]{2,1,0:T(8,128)(2,1)} %perturb_ref.1) | copy-start | bytes 1105924
  1.7 0.8 %copy-start.1 = (f32[512,32]{0,1:T(8,128)S(1)}, f32[512,32]{0,1:T(8,128)}, u32[]{:S(2)}) copy-start(f32[512,32]{0,1:T(8,128)} %param.6) | copy-start | bytes 196612
  2.5 52.7 %copy-start.5 = (bf16[1,1440,128]{2,1,0:T(8,128)(2,1)S(1)}, bf16[1,1440,128]{2,1,0:T(8,128)(2,1)}, u32[]{:S(2)}) copy-start(bf16[1,1440,128]{2,1,0:T(8,128)(2,1)} %param.11) | copy-start | bytes 1105924

commit v3 on v2

--- a/solution.py
+++ b/solution.py
@@ -65,9 +65,10 @@
 
 def body(
     n, mems, owners, part_rows,
-    rows_ref, band_ref, cell_ref, top_ref, perturb_ref,
+    rows_hbm, band_hbm, cell_hbm, top_hbm, perturb_hbm,
     out_ref,
-    msg_ref, obs_ref, rhs_ref, cells_ref, inno_ref, v_ref, got_ref, m_ref, back_ref, g_hi, g_lo,
+    rows_ref, band_ref, cell_ref, top_ref, perturb_ref, in_sem,
+    msg_ref, obs_ref, rhs_ref, cells_ref, inno_ref, v_ref, got_ref, m_ref, back_ref, g_hi, g_lo, both_ref,
     obs_send, obs_recv, mem_send, mem_recv, v_send, v_recv, m_send, m_recv,
 ):
     me, mem = lax.axis_index("lat"), lax.axis_index("mem")
@@ -75,6 +76,17 @@
     levels = rows_ref.shape[0]
     chunk = PARTS * part_rows
 
+    loads = [
+        pltpu.make_async_copy(source, target, in_sem.at[i])
+        for i, (source, target) in enumerate(
+            (
+                (rows_hbm, rows_ref), (band_hbm, band_ref), (cell_hbm, cell_ref),
+                (top_hbm, top_ref), (perturb_hbm, perturb_ref),
+            )
+        )
+    ]
+    for load in loads:
+        load.start()
     barrier = pltpu.get_barrier_semaphore()
 
     def greet(k, carry):
@@ -84,6 +96,8 @@
     lax.fori_loop(1, n, greet, 0)
     for k in range(1, mems):
         pl.semaphore_signal(barrier, inc=1, device_id={"mem": lax.rem(mem + k, mems)})
+    for load in loads[:4]:
+        load.wait()
     make_messages(me, rows_ref, band_ref, cell_ref, top_ref, msg_ref, n)
     pl.semaphore_wait(barrier, n - 1 + mems - 1)
 
@@ -121,7 +135,7 @@
             g_lo[p, pl.ds(start, tile), :] = low
             return carry
 
-        lax.fori_loop(0, lon // tile, rows_of, 0)
+        lax.fori_loop(0, lon // BLOCKS // tile, rows_of, 0)
 
     zonal_kernel(0)
     a, b = iota((columns, columns), 0), iota((columns, columns), 1)
@@ -191,6 +205,7 @@
         low_half = lower == (k >= mid)
         return jnp.where(low_half, 0, mid) + lax.rem(me + k, mid)
 
+    loads[4].wait()
     for step in range(BLOCKS):
         block = jnp.where(lower, BLOCKS - 1 - step, step)
         base = block * block_rows
@@ -287,12 +302,14 @@
                 arrived = back_ref.at[p, pl.ds(0, total)]
                 pltpu.make_async_copy(arrived, arrived, m_recv.at[p]).wait()
 
-        high, low = split(back_ref[p].reshape(half, columns))
-        both = jnp.concatenate([high, low], axis=1)
+        both = jnp.concatenate(split(back_ref[p].reshape(half, columns)), axis=1)
+        both_ref[p, 0:half, :] = both
+        both_ref[p, half : 2 * half, :] = both
         for step in range(BLOCKS):
             rows = pl.ds(step * block_rows, block_rows)
-            wide = dot(g_hi[p, rows, :], both)
-            narrow = dot(g_lo[p, rows, :], high)
+            turn = pl.ds(step * (half // BLOCKS), half)
+            wide = dot(g_hi[p], both_ref[p, turn, :])
+            narrow = dot(g_lo[p], both_ref[p, turn, 0:128])
             total = wide[:, 0:128] + (wide[:, 128:256] + narrow)
             out_ref[0, rows, :] = total if p == 0 else out_ref[0, rows, :] + total
 
@@ -336,9 +353,15 @@
     zonal = pl.pallas_call(
         functools.partial(body, n, mems, owners, part_rows),
         out_shape=jax.ShapeDtypeStruct((1, lon, columns), F32),
-        in_specs=[pl.BlockSpec(memory_space=pltpu.VMEM)] * 5,
+        in_specs=[pl.BlockSpec(memory_space=pltpu.HBM)] * 5,
         out_specs=pl.BlockSpec(memory_space=pltpu.VMEM),
         scratch_shapes=[
+            pltpu.VMEM((levels, count), F32),
+            pltpu.VMEM((1, count), jnp.int32),
+            pltpu.VMEM((1, count), jnp.int32),
+            pltpu.VMEM((1, count), jnp.int32),
+            pltpu.VMEM((1, lon, columns), BF16),
+            pltpu.SemaphoreType.DMA((5,)),
             pltpu.VMEM((n, 16, 128), F32),
             pltpu.VMEM((mems, n, 16, 128), F32),
             pltpu.VMEM((depth, 128 * QUADS, 256), BF16),
@@ -348,13 +371,14 @@
             pltpu.VMEM((PARTS, n, part_rows, columns), F32),
             pltpu.VMEM((PARTS, n, part_rows, columns), F32),
             pltpu.VMEM((PARTS, owners, part_rows, columns), F32),
-            pltpu.VMEM((PARTS, lon, half), BF16),
-            pltpu.VMEM((PARTS, lon, half), BF16),
+            pltpu.VMEM((PARTS, lon // BLOCKS, half), BF16),
+            pltpu.VMEM((PARTS, lon // BLOCKS, half), BF16),
+            pltpu.VMEM((PARTS, 2 * half, 256), BF16),
             dma((n,)), dma(()), dma((mems,)), dma((mems,)),
             dma((PARTS, n)), dma((PARTS,)), dma((PARTS, n)), dma((PARTS,)),
         ],
         compiler_params=pltpu.CompilerParams(
-            collective_id=0, has_side_effects=True, vmem_limit_bytes=30 * 1024 * 1024
+            collective_id=0, has_side_effects=True, vmem_limit_bytes=56 * 1024 * 1024
         ),
     )(
         obs_rows.T, obs_band.reshape(1, count), obs_cell.reshape(1, count),

time: 56.4 us -> 55.9 us (level)
  local copies, waits for them, and re-layouts: 2.54 us -> 0.01 us
  other arithmetic: 0.93 us -> 2.04 us
  Pallas kernels: 52.7 us -> 53.7 us
    unnamed x12 -> x2, local copies, waits for them, and re-layouts: 2.54 us -> 0.01 us
    add x1, other arithmetic: 0.93 us -> 2.04 us  [local(): return control.astype(F32) + zonal]
    pallas_call x1, Pallas kernels: 52.7 us -> 53.7 us  [local(): pl.pallas_call(functools.partial(body, n, mems, owners, part_rows), out_s...]
where the time goes in v3:
time: 55.9 us; the launch traced here: 55.7 us
  Pallas kernels  53.7 us (96%)
  other arithmetic  2.04 us (4%)
    pallas_call x1, Pallas kernels, local(): pl.pallas_call(functools.partial(body, n, mems, owners, part_rows), out_s...  53.7 us
    add x1, other arithmetic, local(): return control.astype(F32) + zonal  2.04 us

profile of v3, /device:TPU:0, one launch (start us, length us, event | category | flops | bytes accessed | tf_op | source)
XLA Modules:
  0.0 55.7 jit_solution(310372558854297239)
XLA Ops:
  0.0 0.0 copy-start
  0.0 53.7 %shard_map.64 = f32[1,1440,128]{2,1,0:T(8,128)} custom-call(f32[32,512]{1,0:T(8,128)} %bitcast.4, s32[1,512]{1,0:T(1,128)} %bitcast.5, s32[1,512]{1,0:T(1,128)} %bitcast.6, s32[1,512]{1,0:T(1,128)} %bitcast.7, bf16[1,1440,128]{2,1,0:T(8,128)(2,1)} %perturb_hbm.1), custom_call_target="tpu_custom_call" | custom-call | tf_op jit(solution)/shard_map/pallas_call | solution.py:353
  53.7 0.0 copy-done
  53.7 2.0 %convert_add_fusion = f32[1,1440,128]{2,1,0:T(8,128)} fusion(f32[1,1440,128]{2,1,0:T(8,128)} %shard_map.64, bf16[1,1440,128]{2,1,0:T(8,128)(2,1)S(1)} %copy-done), kind=kLoop, calls=%fused_computation | loop fusion | flops 368640 | bytes 1843200 | tf_op jit(solution)/shard_map/add | solution.py:387
Async XLA Ops:
  0.0 53.7 %copy-start = (bf16[1,1440,128]{2,1,0:T(8,128)(2,1)S(1)}, bf16[1,1440,128]{2,1,0:T(8,128)(2,1)}, u32[]{:S(2)}) copy-start(bf16[1,1440,128]{2,1,0:T(8,128)(2,1)} %param.11) | copy-start | bytes 1105924

commit v4 on v3

--- a/solution.py
+++ b/solution.py
@@ -10,7 +10,7 @@
 from jax.sharding import PartitionSpec as P
 
 CAP = 32
-PARTS = 3
+PARTS = 6
 BLOCKS = 3
 QUADS = 4
 F32 = jnp.float32
@@ -68,7 +68,7 @@
     rows_hbm, band_hbm, cell_hbm, top_hbm, perturb_hbm,
     out_ref,
     rows_ref, band_ref, cell_ref, top_ref, perturb_ref, in_sem,
-    msg_ref, obs_ref, rhs_ref, cells_ref, inno_ref, v_ref, got_ref, m_ref, back_ref, g_hi, g_lo, both_ref,
+    msg_ref, obs_ref, rhs_ref, cells_ref, inno_ref, v_ref, got_ref, m_ref, back_ref, g_hi, g_lo, both_ref, sum_ref, out_sem,
     obs_send, obs_recv, mem_send, mem_recv, v_send, v_recv, m_send, m_recv,
 ):
     me, mem = lax.axis_index("lat"), lax.axis_index("mem")
@@ -294,6 +294,10 @@
             lax.fori_loop(mid + 1, n, start_m, 0)
             back_ref[p, me] = m_ref[p, me]
 
+    def out_copy(step):
+        rows = pl.ds(step * block_rows, block_rows)
+        return pltpu.make_async_copy(sum_ref.at[rows], out_ref.at[0, rows], out_sem.at[step])
+
     for p in range(PARTS):
         for own, total in ((True, owners - 1), (False, owners)):
 
@@ -311,13 +315,17 @@
             wide = dot(g_hi[p], both_ref[p, turn, :])
             narrow = dot(g_lo[p], both_ref[p, turn, 0:128])
             total = wide[:, 0:128] + (wide[:, 128:256] + narrow)
-            out_ref[0, rows, :] = total if p == 0 else out_ref[0, rows, :] + total
+            sum_ref[rows, :] = total if p == 0 else sum_ref[rows, :] + total
+            if p == PARTS - 1:
+                out_copy(step).start()
 
     def end_obs(k, carry):
         obs_copy(k).wait_send()
         return carry
 
     lax.fori_loop(1, n, end_obs, 0)
+    for step in range(BLOCKS):
+        out_copy(step).wait()
     for p in range(PARTS):
 
         def end_v(dest, carry):
@@ -354,7 +362,7 @@
         functools.partial(body, n, mems, owners, part_rows),
         out_shape=jax.ShapeDtypeStruct((1, lon, columns), F32),
         in_specs=[pl.BlockSpec(memory_space=pltpu.HBM)] * 5,
-        out_specs=pl.BlockSpec(memory_space=pltpu.VMEM),
+        out_specs=pl.BlockSpec(memory_space=pltpu.HBM),
         scratch_shapes=[
             pltpu.VMEM((levels, count), F32),
             pltpu.VMEM((1, count), jnp.int32),
@@ -374,6 +382,8 @@
             pltpu.VMEM((PARTS, lon // BLOCKS, half), BF16),
             pltpu.VMEM((PARTS, lon // BLOCKS, half), BF16),
             pltpu.VMEM((PARTS, 2 * half, 256), BF16),
+            pltpu.VMEM((lon, columns), F32),
+            pltpu.SemaphoreType.DMA((BLOCKS,)),
             dma((n,)), dma(()), dma((mems,)), dma((mems,)),
             dma((PARTS, n)), dma((PARTS,)), dma((PARTS, n)), dma((PARTS,)),
         ],

time: 55.9 us -> 56.9 us (1.018)
  Pallas kernels: 53.7 us -> 54.7 us
    pallas_call x1, Pallas kernels: 53.7 us -> 54.7 us  [local(): pl.pallas_call(functools.partial(body, n, mems, owners, part_rows), out_s...]
where the time goes in v4:
time: 56.9 us; the launch traced here: 56.7 us
  Pallas kernels  54.7 us (96%)
  other arithmetic  2.04 us (4%)
    pallas_call x1, Pallas kernels, local(): pl.pallas_call(functools.partial(body, n, mems, owners, part_rows), out_s...  54.7 us
    add x1, other arithmetic, local(): return control.astype(F32) + zonal  2.04 us

profile of v4, /device:TPU:0, one launch (start us, length us, event | category | flops | bytes accessed | tf_op | source)
XLA Modules:
  0.0 56.7 jit_solution(5039586674817093650)
XLA Ops:
  0.0 0.0 copy-start
  0.0 54.7 %shard_map.64 = f32[1,1440,128]{2,1,0:T(8,128)} custom-call(f32[32,512]{1,0:T(8,128)} %bitcast.4, s32[1,512]{1,0:T(1,128)} %bitcast.5, s32[1,512]{1,0:T(1,128)} %bitcast.6, s32[1,512]{1,0:T(1,128)} %bitcast.7, bf16[1,1440,128]{2,1,0:T(8,128)(2,1)} %perturb_hbm.1), custom_call_target="tpu_custom_call" | custom-call | tf_op jit(solution)/shard_map/pallas_call | solution.py:361
  54.7 0.0 copy-done
  54.7 2.0 %convert_add_fusion = f32[1,1440,128]{2,1,0:T(8,128)} fusion(f32[1,1440,128]{2,1,0:T(8,128)} %shard_map.64, bf16[1,1440,128]{2,1,0:T(8,128)(2,1)S(1)} %copy-done), kind=kLoop, calls=%fused_computation | loop fusion | flops 368640 | bytes 1843200 | tf_op jit(solution)/shard_map/add | solution.py:397
Async XLA Ops:
  0.0 54.7 %copy-start = (bf16[1,1440,128]{2,1,0:T(8,128)(2,1)S(1)}, bf16[1,1440,128]{2,1,0:T(8,128)(2,1)}, u32[]{:S(2)}) copy-start(bf16[1,1440,128]{2,1,0:T(8,128)(2,1)} %param.11) | copy-start | bytes 1105924
